TPU v7x, 32 devices: a whole 2x2x4 slice. The times are simulated.
32 devices in a mesh: orb: 8 (over z, core), aux: 4 (over y, x).
Axes of the slice: x: 2, y: 2, z: 4, core: 2. Of those that a mesh axis runs over, the one named last changes fastest.
Arguments:
- three_centre: bfloat16 [32, 4096, 384], P('aux', 'orb'), may hold values from -6 to 6
- b_screen: int32 [32, 3], P('orb'), may hold values 0 or 1
- g_occ: bfloat16 [4096, 384], P('orb'), may hold values from -0.0068359375 to 0.0068359375
- occ_screen: int32 [32, 3], P('orb'), may hold values 0 or 1
- g_vir: bfloat16 [4096, 384], P('orb'), may hold values from -0.0068359375 to 0.0068359375
- vir_screen: int32 [32, 3], P('orb'), may hold values 0 or 1
Outputs:
- response: float32 [32, 32], P('aux')
All inputs are finite; a program needn't handle non-finite values. No bound on the sum of `b_screen` or of `occ_screen` or of `vir_screen` on one device may be relied on, other than what follows from the above.
Results may differ from a plain program's by a relative error of at most 0.0029.
Values may be sent and summed in bfloat16 or wider, within the bound.
A program may use at most 128 MiB of HBM per device.

v0:
```python
import jax
import jax.numpy as jnp
from jax import lax
from jax.sharding import PartitionSpec as P


def with_halo(block, sides, width):
    for axis, dim in sides:
        count = lax.axis_size(axis)
        forward = [(i, i + 1) for i in range(count - 1)]
        backward = [(target, source) for source, target in forward]
        low = lax.ppermute(
            lax.slice_in_dim(block, block.shape[dim] - width, None, axis=dim), axis, forward
        )
        high = lax.ppermute(lax.slice_in_dim(block, 0, width, axis=dim), axis, backward)
        block = jnp.concatenate([low, block, high], axis=dim)
    return block


def tile_mask(screen, first, nob, block_size):
    count = screen.shape[0]
    blocks = (
        first
        + jnp.arange(count, dtype=jnp.int32)[:, None]
        + jnp.arange(3, dtype=jnp.int32)[None, :]
        - 1
    )
    live = (screen == 1) & (blocks >= 0) & (blocks < nob)
    return jnp.repeat(jnp.repeat(live, block_size, axis=0), block_size, axis=1)


def per_device(three_centre, b_screen, g_occ, occ_screen, g_vir, vir_screen):
    aux_dev, rows, width = three_centre.shape
    block_size = width // 3
    nbd = rows // block_size
    nob = nbd * lax.axis_size("orb")
    first = lax.axis_index("orb") * nbd
    nothing = jnp.zeros((), jnp.bfloat16)
    every_b = lax.all_to_all(three_centre, "aux", split_axis=1, concat_axis=0, tiled=True)
    b_mask = tile_mask(b_screen, first, nob, block_size)[None]
    kept_b = jnp.where(b_mask, three_centre, nothing)
    kept_o = jnp.where(tile_mask(occ_screen, first, nob, block_size), g_occ, nothing)
    kept_v = jnp.where(tile_mask(vir_screen, first, nob, block_size), g_vir, nothing)
    wide_b = with_halo(kept_b, (("orb", 1),), block_size)
    wide_v = with_halo(kept_v, (("orb", 0),), block_size)
    right = jnp.zeros((aux_dev, nbd, block_size, 5 * block_size), jnp.float32)
    for slot in range(3):
        lower = slot * block_size
        occ_slot = kept_o[:, lower : lower + block_size].reshape(nbd, block_size, block_size)
        near_b = wide_b[:, lower : lower + rows].reshape(aux_dev, nbd, block_size, width)
        term = jnp.einsum("jin,qjnk->qjik", occ_slot, near_b, preferred_element_type=jnp.float32)
        right = right.at[..., lower : lower + width].add(term)
    right_b = right.astype(jnp.bfloat16)
    parts = []
    for slot in range(3):
        lower = slot * block_size
        vir_rows = wide_v[lower : lower + rows].reshape(nbd, block_size, width)
        parts.append(
            jnp.einsum(
                "qjik,jlk->qjil",
                right_b[..., lower : lower + width],
                vir_rows,
                preferred_element_type=jnp.float32,
            )
        )
    w = jnp.concatenate(parts, axis=-1).reshape(aux_dev, rows, width)
    w = jnp.where(b_mask, w, 0.0).astype(jnp.bfloat16)
    every_w = lax.all_to_all(w, "aux", split_axis=1, concat_axis=0, tiled=True)
    partial_value = lax.dot_general(
        every_b, every_w, (((1, 2), (1, 2)), ((), ())), preferred_element_type=jnp.float32
    )
    summed = lax.psum(partial_value, ("orb", "aux"))
    return lax.dynamic_slice_in_dim(summed, lax.axis_index("aux") * aux_dev, aux_dev, 0)


def solution(mesh):
    in_specs = (
        P("aux", "orb", None),
        P("orb", None),
        P("orb", None),
        P("orb", None),
        P("orb", None),
        P("orb", None),
    )
    out_specs = P("aux", None)
    return jax.shard_map(
        per_device, mesh=mesh, in_specs=in_specs, out_specs=out_specs, check_vma=False
    )
```

profile of v0, /device:TPU:0, one launch (start us, length us, event | category | flops | bytes accessed | tf_op | source)
XLA Modules:
  0.0 161.0 jit_solution(2481949846016735281)
XLA Ops:
  0.0 0.8 and_and_fusion.2
  0.8 0.1 copy.36
  0.9 0.1 broadcast_bitcast_fusion.2
  1.1 0.3 copy.37
  1.4 2.5 %broadcast_select_fusion = bf16[8,512,384]{2,1,0:T(8,128)(2,1)S(1)} fusion(bf16[8,512,384]{2,1,0:T(8,128)(2,1)} %param.12, pred[512,384]{1,0:T(8,128)(4,1)S(1)} %copy.37), kind=kLoop, calls=%fused_computation.26 | loop fusion | flops 1572864 | bytes 6488064 | tf_op jit(solution)/shard_map/jit(_where)/select_n | solution.py:41
  3.9 1.4 fusion.43
  5.2 3.2 %collective-permute-start.1 = (bf16[8,128,384]{2,1,0:T(8,128)(2,1)}, bf16[8,128,384]{2,1,0:T(8,128)(2,1)}, u32[]{:S(2)}, u32[]{:S(2)}) collective-permute-start(bf16[8,128,384]{2,1,0:T(8,128)(2,1)} %get-tuple-element.44), channel_id=1, source_target_pairs={{0,4},{4,8},{8,12},{12,16},{16,20},{20,24},{24,28},{1,5},{5,9},{9,... | collective-permute-start | bytes 2359304 | tf_op jit(solution)/shard_map/ppermute | solution.py:12
  8.5 1.3 collective-permute-start.2
  9.8 0.1 copy.38
  9.9 0.1 broadcast_bitcast_fusion.1
  10.0 1.9 %copy.39 = bf16[512,384]{0,1:T(8,128)(2,1)} copy(bf16[512,384]{1,0:T(8,128)(2,1)} %param.16) | data formatting | bytes 786432 | tf_op args[4]
  11.9 1.0 bitcast_select_fusion.2
  12.9 0.7 fusion.44
  13.6 5.0 %collective-permute-start = (bf16[128,384]{0,1:T(8,128)(2,1)}, bf16[128,384]{0,1:T(8,128)(2,1)}, u32[]{:S(2)}, u32[]{:S(2)}) collective-permute-start(bf16[128,384]{0,1:T(8,128)(2,1)} %get-tuple-element.47), channel_id=1, source_target_pairs={{0,4},{4,8},{8,12},{12,16},{16,20},{20,24},{24,28},{1,5},{5,9},{9,... | collective-permute-start | bytes 294920 | tf_op jit(solution)/shard_map/ppermute | solution.py:12
  18.6 1.3 collective-permute-start.3
  19.9 5.4 %copy.57 = bf16[8,512,384]{2,0,1:T(8,128)(2,1)} copy(bf16[8,512,384]{2,1,0:T(8,128)(2,1)} %param.12) | data formatting | bytes 6291456 | tf_op args[0]
  25.4 4.7 %all-to-all-start.1 = ((bf16[8,512,384]{2,0,1:T(8,128)(2,1)}), bf16[8,512,384]{2,0,1:T(8,128)(2,1)}, u32[]{:S(2)}, u32[]{:S(2)}) async-start(bf16[8,512,384]{2,0,1:T(8,128)(2,1)} %copy.57), calls=%async_computation.1 | async-start | bytes 6291456 | tf_op jit(solution)/shard_map/all_to_all | solution.py:39
  30.0 0.1 copy.41
  30.1 0.1 broadcast_bitcast_fusion
  30.2 1.9 %copy.42 = bf16[512,384]{0,1:T(8,128)(2,1)} copy(bf16[512,384]{1,0:T(8,128)(2,1)} %param.14) | data formatting | bytes 786432 | tf_op args[2]
  32.2 1.0 bitcast_select_fusion.1
  33.2 0.8 fusion.45
  34.0 0.9 copy.75
  34.9 1.7 %copy.43 = bf16[512,128]{1,0:T(8,128)(2,1)} copy(bf16[512,128]{0,1:T(8,128)(2,1)} %get-tuple-element.51) | data formatting | bytes 262144 | tf_op jit(solution)/shard_map/slice | solution.py:49
  36.5 1.7 %copy.45 = bf16[512,128]{1,0:T(8,128)(2,1)} copy(bf16[512,128]{0,1:T(8,128)(2,1)} %get-tuple-element.50) | data formatting | bytes 262144 | tf_op jit(solution)/shard_map/slice | solution.py:49
  38.2 1.7 %copy.47 = bf16[512,128]{1,0:T(8,128)(2,1)} copy(bf16[512,128]{0,1:T(8,128)(2,1)} %get-tuple-element.49) | data formatting | bytes 262144 | tf_op jit(solution)/shard_map/slice | solution.py:49
  39.9 1.9 %pad_maximum_fusion.4 = (bf16[512,384]{0,1:T(8,128)(2,1)}, bf16[512,384]{0,1:T(8,128)(2,1)}) fusion(bf16[512,384]{0,1:T(8,128)(2,1)S(1)} %bitcast_select_fusion.2, bf16[128,384]{0,1:T(8,128)(2,1)} %collective-permute-done, bf16[128,384]{0,1:T(8,128)(2,1)} %collective-permute-done.3), kind=kLoop, calls=%fused_computation.35 | loop fusion | flops 1572864 | bytes 1376256 | tf_op jit(solution)/shard_map/concatenate | solution.py:16
  41.8 1.2 copy.40
  43.0 1.9 %copy.52 = bf16[512,384]{1,0:T(8,128)(2,1)} copy(bf16[512,384]{0,1:T(8,128)(2,1)} %get-tuple-element.46) | data formatting | bytes 786432 | tf_op jit(solution)/shard_map/slice | solution.py:57
  44.9 3.1 %pad_maximum_fusion.1 = (bf16[8,512,384]{2,1,0:T(8,128)(2,1)}, bf16[8,512,384]{2,1,0:T(8,128)(2,1)S(1)}) fusion(bf16[8,128,384]{2,1,0:T(8,128)(2,1)} %collective-permute-done.2, bf16[8,512,384]{2,1,0:T(8,128)(2,1)S(1)} %broadcast_select_fusion, bf16[8,128,384]{2,1,0:T(8,128)(2,1)} %collective-permute-done.1), kind=kLoop, calls=%fused_computation.13 | loop fusion | flops 12582912 | bytes 11010048 | tf_op jit(solution)/shard_map/concatenate | solution.py:16
  48.0 1.2 fusion.24
  49.3 1.5 scatter-add.10
  50.8 3.3 %fusion.2 = f32[8,4,128,640]{2,3,0,1:T(8,128)S(1)} fusion(f32[8,4,128,640]{2,3,0,1:T(8,128)S(1)} %scatter-add.10, bf16[4,128,128,1]{2,1,3,0:T(8,128)(2,1)S(1)} %bitcast.109, bf16[8,4,128,384]{3,2,1,0:T(8,128)(2,1)S(1)} %bitcast.103), kind=kOutput, calls=%fused_computation.6 | convolution fusion | flops 404226048 | bytes 15859712 | tf_op jit(solution)/shard_map/jin,qjnk->qjik/dot_general | solution.py:51
  54.1 3.3 %fusion = f32[8,4,128,640]{2,3,0,1:T(8,128)S(1)} fusion(f32[8,4,128,640]{2,3,0,1:T(8,128)S(1)} %fusion.2, bf16[4,128,128,1]{2,1,3,0:T(8,128)(2,1)S(1)} %bitcast.108, bf16[8,4,128,384]{3,2,1,0:T(8,128)(2,1)S(1)} %bitcast.105), kind=kOutput, calls=%fused_computation.1 | convolution fusion | flops 404226048 | bytes 15859712 | tf_op jit(solution)/shard_map/jin,qjnk->qjik/dot_general | solution.py:51
  57.3 3.1 %convert_element_type.6 = bf16[8,4,128,640]{2,3,0,1:T(8,128)(2,1)} convert(f32[8,4,128,640]{2,3,0,1:T(8,128)S(1)} %fusion) | non-fusion elementwise | flops 2621440 | bytes 15728640 | tf_op jit(solution)/shard_map/convert_element_type | solution.py:53
  60.5 2.8 %fusion.27 = bf16[8,4,128,128]{2,3,0,1:T(8,128)(2,1)S(1)} fusion(bf16[4,128,384,1]{2,1,3,0:T(8,128)(2,1)S(1)} %bitcast.112, bf16[8,4,128,640]{2,3,0,1:T(8,128)(2,1)} %convert_element_type.6), kind=kOutput, calls=%fused_computation.28 | convolution fusion | flops 402653184 | bytes 4587520 | tf_op jit(solution)/shard_map/qjik,jlk->qjil/dot_general | solution.py:59
  63.2 2.7 %fusion.33 = bf16[8,4,128,128]{2,3,0,1:T(8,128)(2,1)S(1)} fusion(bf16[4,128,384,1]{2,1,3,0:T(8,128)(2,1)S(1)} %bitcast.113, bf16[8,4,128,640]{2,3,0,1:T(8,128)(2,1)} %convert_element_type.6), kind=kOutput, calls=%fused_computation.30 | convolution fusion | flops 402653184 | bytes 4587520 | tf_op jit(solution)/shard_map/qjik,jlk->qjil/dot_general | solution.py:59
  65.9 0.7 fusion.30
  66.7 0.3 pad_maximum_fusion
  67.0 2.8 %copy.54 = bf16[8,4,128,384]{3,2,1,0:T(8,128)(2,1)} copy(bf16[8,4,128,384]{2,3,0,1:T(8,128)(2,1)S(1)} %pad_maximum_fusion) | data formatting | bytes 6291456 | tf_op jit(solution)/shard_map/concatenate | solution.py:66
  69.8 2.5 %fusion.1 = bf16[8,512,384]{2,1,0:T(8,128)(2,1)S(1)} fusion(bf16[8,4,128,384]{3,2,1,0:T(8,128)(2,1)} %copy.54, pred[512,384]{1,0:T(8,128)(4,1)S(1)} %copy-done.3), kind=kLoop, calls=%fused_computation.4 | loop fusion | flops 1572864 | bytes 6488064 | tf_op jit(solution)/shard_map/convert_element_type | solution.py:67
  72.4 3.5 %copy.55 = bf16[8,512,384]{2,0,1:T(8,128)(2,1)} copy(bf16[8,512,384]{2,1,0:T(8,128)(2,1)S(1)} %fusion.1) | data formatting | bytes 6291456 | tf_op jit(solution)/shard_map/convert_element_type | solution.py:67
  75.9 4.2 %all-to-all-start = ((bf16[8,512,384]{2,0,1:T(8,128)(2,1)}), bf16[8,512,384]{2,0,1:T(8,128)(2,1)S(1)}, u32[]{:S(2)}, u32[]{:S(2)}) async-start(bf16[8,512,384]{2,0,1:T(8,128)(2,1)} %copy.55), calls=%async_computation | async-start | bytes 6291456 | tf_op jit(solution)/shard_map/all_to_all | solution.py:68
  80.0 37.2 %all-to-all-done = bf16[8,512,384]{2,0,1:T(8,128)(2,1)S(1)} async-done(((bf16[8,512,384]{2,0,1:T(8,128)(2,1)}), bf16[8,512,384]{2,0,1:T(8,128)(2,1)S(1)}, u32[]{:S(2)}, u32[]{:S(2)}) %all-to-all-start) | async-done | bytes 3145760 | tf_op jit(solution)/shard_map/all_to_all | solution.py:68
  117.3 2.8 %fusion.36 = f32[32,32]{0,1:T(8,128)S(1)} fusion(bf16[8,4,128,384]{3,0,2,1:T(8,128)(2,1)} %bitcast.34, bf16[8,4,128,384]{3,0,2,1:T(8,128)(2,1)S(1)} %bitcast.106), kind=kOutput, calls=%fused_computation.31 | convolution fusion | flops 100663296 | bytes 6295552 | tf_op jit(solution)/shard_map/dot_general | solution.py:69
  120.1 40.1 %psum.7 = f32[32,32]{0,1:T(8,128)S(1)} all-reduce(f32[32,32]{0,1:T(8,128)S(1)} %fusion.36), channel_id=1, replica_groups=mesh['orb'=8,'aux'=4] {'orb','aux'}, use_global_device_ids=true, to_apply=%region_0.1 | all-reduce | flops 1024 | bytes 8192 | tf_op jit(solution)/shard_map/psum | solution.py:72
  160.2 0.1 constant_dynamic-slice_fusion
  160.3 0.7 copy.59
  (28 shorter events, 0.1 us)
Async XLA Ops:
  1.4 2.5 %copy-start.2 = (pred[512,384]{1,0:T(8,128)(4,1)}, pred[512,384]{1,0:T(8,128)(4,1)S(1)}, u32[]{:S(2)}) copy-start(pred[512,384]{1,0:T(8,128)(4,1)S(1)} %copy.37) | copy-start | bytes 589828
  5.2 39.7 %collective-permute-start.1 = (bf16[8,128,384]{2,1,0:T(8,128)(2,1)}, bf16[8,128,384]{2,1,0:T(8,128)(2,1)}, u32[]{:S(2)}, u32[]{:S(2)}) collective-permute-start(bf16[8,128,384]{2,1,0:T(8,128)(2,1)} %get-tuple-element.44), channel_id=1, source_target_pairs={{0,4},{4,8},{8,12},{12,16},{16,20},{20,24},{24,28},{1,5},{5,9},{9,... | collective-permute-start | bytes 2359304 | tf_op jit(solution)/shard_map/ppermute | solution.py:12
  8.5 36.4 %collective-permute-start.2 = (bf16[8,128,384]{2,1,0:T(8,128)(2,1)}, bf16[8,128,384]{2,1,0:T(8,128)(2,1)}, u32[]{:S(2)}, u32[]{:S(2)}) collective-permute-start(bf16[8,128,384]{2,1,0:T(8,128)(2,1)} %get-tuple-element.43), channel_id=1, source_target_pairs={{4,0},{8,4},{12,8},{16,12},{20,16},{24,20},{28,24},{5,1},{9,5},{13... | collective-permute-start | bytes 2359304 | tf_op jit(solution)/shard_map/ppermute | solution.py:15
  13.6 26.2 %collective-permute-start = (bf16[128,384]{0,1:T(8,128)(2,1)}, bf16[128,384]{0,1:T(8,128)(2,1)}, u32[]{:S(2)}, u32[]{:S(2)}) collective-permute-start(bf16[128,384]{0,1:T(8,128)(2,1)} %get-tuple-element.47), channel_id=1, source_target_pairs={{0,4},{4,8},{8,12},{12,16},{16,20},{20,24},{24,28},{1,5},{5,9},{9,... | collective-permute-start | bytes 294920 | tf_op jit(solution)/shard_map/ppermute | solution.py:12
  18.6 21.2 %collective-permute-start.3 = (bf16[128,384]{0,1:T(8,128)(2,1)}, bf16[128,384]{0,1:T(8,128)(2,1)}, u32[]{:S(2)}, u32[]{:S(2)}) collective-permute-start(bf16[128,384]{0,1:T(8,128)(2,1)} %get-tuple-element.48), channel_id=1, source_target_pairs={{4,0},{8,4},{12,8},{16,12},{20,16},{24,20},{28,24},{5,1},{9,5},{13... | collective-permute-start | bytes 294920 | tf_op jit(solution)/shard_map/ppermute | solution.py:15
  25.4 50.5 %all-to-all-start.1 = ((bf16[8,512,384]{2,0,1:T(8,128)(2,1)}), bf16[8,512,384]{2,0,1:T(8,128)(2,1)}, u32[]{:S(2)}, u32[]{:S(2)}) async-start(bf16[8,512,384]{2,0,1:T(8,128)(2,1)} %copy.57), calls=%async_computation.1 | async-start | bytes 6291456 | tf_op jit(solution)/shard_map/all_to_all | solution.py:39
  44.9 3.1 %copy-start.6 = (bf16[512,128]{1,0:T(8,128)(2,1)S(1)}, bf16[512,128]{1,0:T(8,128)(2,1)}, u32[]{:S(2)}) copy-start(bf16[512,128]{1,0:T(8,128)(2,1)} %copy.43) | copy-start | bytes 393220
  49.3 1.5 copy-start.5
  50.8 3.3 %copy-start = (bf16[8,512,384]{2,1,0:T(8,128)(2,1)S(1)}, bf16[8,512,384]{2,1,0:T(8,128)(2,1)}, u32[]{:S(2)}) copy-start(bf16[8,512,384]{2,1,0:T(8,128)(2,1)} %get-tuple-element.41) | copy-start | bytes 9437188
  50.8 3.3 %copy-start.4 = (bf16[512,128]{1,0:T(8,128)(2,1)S(1)}, bf16[512,128]{1,0:T(8,128)(2,1)}, u32[]{:S(2)}) copy-start(bf16[512,128]{1,0:T(8,128)(2,1)} %copy.47) | copy-start | bytes 393220
  60.5 2.8 %copy-start.8 = (bf16[512,384]{1,0:T(8,128)(2,1)S(1)}, bf16[512,384]{1,0:T(8,128)(2,1)}, u32[]{:S(2)}) copy-start(bf16[512,384]{1,0:T(8,128)(2,1)} %copy.52) | copy-start | bytes 1179652
  60.5 5.5 %copy-start.1 = (bf16[8,4,128,640]{2,3,0,1:T(8,128)(2,1)S(1)}, bf16[8,4,128,640]{2,3,0,1:T(8,128)(2,1)}, u32[]{:S(2)}) copy-start(bf16[8,4,128,640]{2,3,0,1:T(8,128)(2,1)} %convert_element_type.6) | copy-start | bytes 15728644
  63.2 2.7 %copy-start.7 = (bf16[512,384]{1,0:T(8,128)(2,1)S(1)}, bf16[512,384]{1,0:T(8,128)(2,1)}, u32[]{:S(2)}) copy-start(bf16[512,384]{1,0:T(8,128)(2,1)} %copy.75) | copy-start | bytes 1179652
  67.0 2.8 %copy-start.3 = (pred[512,384]{1,0:T(8,128)(4,1)S(1)}, pred[512,384]{1,0:T(8,128)(4,1)}, u32[]{:S(2)}) copy-start(pred[512,384]{1,0:T(8,128)(4,1)} %copy-done.2) | copy-start | bytes 589828
  75.9 41.4 %all-to-all-start = ((bf16[8,512,384]{2,0,1:T(8,128)(2,1)}), bf16[8,512,384]{2,0,1:T(8,128)(2,1)S(1)}, u32[]{:S(2)}, u32[]{:S(2)}) async-start(bf16[8,512,384]{2,0,1:T(8,128)(2,1)} %copy.55), calls=%async_computation | async-start | bytes 6291456 | tf_op jit(solution)/shard_map/all_to_all | solution.py:68
where the time goes:
time: 162 us; the launch traced here: 161 us
  blocking collectives  40.1 us (25%)
  waiting for transfers between devices  37.3 us (23%)
  local copies, waits for them, and re-layouts  30.7 us (19%)
  starting transfers between devices  19.6 us (12%)
  matrix products  16.7 us (10%)
  other arithmetic  16.3 us (10%)
    psum x1, blocking collectives, per_device(): summed = lax.psum(partial_value, ('orb', 'aux'))  40.1 us
    all_to_all x1, waiting for transfers between devices, per_device(): every_w = lax.all_to_all(w, 'aux', split_axis=1, concat_axis=0, tiled=True)  37.2 us
    unnamed x27, local copies, waits for them, and re-layouts  9.6 us
    ppermute x2, starting transfers between devices, with_halo(): lax.ppermute(lax.slice_in_dim(block, block.shape[dim] - width, None, axis...  8.24 us
    dot_general x3, matrix products, per_device(): jnp.einsum('jin,qjnk->qjik', occ_slot, near_b, preferred_element_type=jnp...  7.75 us
    dot_general x3, matrix products, per_device(): jnp.einsum('qjik,jlk->qjil', right_b[..., lower:lower + width], vir_rows,...  6.14 us
    slice x4, local copies, waits for them, and re-layouts, per_device(): kept_o[:, lower:lower + block_size].reshape(nbd, block_size, block_size)  5.76 us
    concatenate x2, other arithmetic, with_halo(): block = jnp.concatenate([low, block, high], axis=dim)  5.03 us
  transfers between devices with their start and end apart: 6, of which 1 were waited for; matrix products, arithmetic and copies ran while one was open for 34% of the time, Pallas kernels for 0%

commit v1 on v0

--- a/solution.py
+++ b/solution.py
@@ -69,7 +69,7 @@
     partial_value = lax.dot_general(
         every_b, every_w, (((1, 2), (1, 2)), ((), ())), preferred_element_type=jnp.float32
     )
-    summed = lax.psum(partial_value, ("orb", "aux"))
+    summed = jnp.sum(lax.all_gather(partial_value, ("orb", "aux")), axis=0)
     return lax.dynamic_slice_in_dim(summed, lax.axis_index("aux") * aux_dev, aux_dev, 0)
 
 

time: 162 us -> 190 us (1.17)
  blocking collectives: 40.1 us -> 68.7 us
    all_gather x0 -> x1, blocking collectives: none -> 68.7 us  [per_device(): summed = jnp.sum(lax.all_gather(partial_value, ('orb', 'aux')), axis=0)]
    psum x1 -> x0, blocking collectives: 40.1 us -> none  [per_device(): summed = lax.psum(partial_value, ('orb', 'aux'))]
  transfers between devices with their start and end apart: 6 -> 6, of which waited for: 1 -> 1; matrix products, arithmetic and copies ran while one was open for 34% -> 29% of each run, Pallas kernels for 0% -> 0%
where the time goes in v1:
time: 190 us
  blocking collectives  68.7 us (36%)
  waiting for transfers between devices  37.3 us (20%)
  local copies, waits for them, and re-layouts  30.7 us (16%)
  starting transfers between devices  19.6 us (10%)
  matrix products  16.7 us (9%)
  other arithmetic  16.4 us (9%)
    all_gather x1, blocking collectives, per_device(): summed = jnp.sum(lax.all_gather(partial_value, ('orb', 'aux')), axis=0)  68.7 us
    all_to_all x1, waiting for transfers between devices, per_device(): every_w = lax.all_to_all(w, 'aux', split_axis=1, concat_axis=0, tiled=True)  37.2 us
    unnamed x27, local copies, waits for them, and re-layouts  9.6 us
    ppermute x2, starting transfers between devices, with_halo(): lax.ppermute(lax.slice_in_dim(block, block.shape[dim] - width, None, axis...  8.24 us
    dot_general x3, matrix products, per_device(): jnp.einsum('jin,qjnk->qjik', occ_slot, near_b, preferred_element_type=jnp...  7.75 us
    dot_general x3, matrix products, per_device(): jnp.einsum('qjik,jlk->qjil', right_b[..., lower:lower + width], vir_rows,...  6.14 us
    slice x4, local copies, waits for them, and re-layouts, per_device(): kept_o[:, lower:lower + block_size].reshape(nbd, block_size, block_size)  5.76 us
    concatenate x2, other arithmetic, with_halo(): block = jnp.concatenate([low, block, high], axis=dim)  5.03 us
  transfers between devices with their start and end apart: 6, of which 1 were waited for; matrix products, arithmetic and copies ran while one was open for 29% of the time, Pallas kernels for 0%

profile of v1, /device:TPU:0, one launch (start us, length us, event | category | flops | bytes accessed | tf_op | source)
XLA Modules:
  0.0 189.5 jit_solution(12322322102036500226)
XLA Ops:
  0.0 0.8 and_and_fusion.2
  0.8 0.1 copy.34
  0.9 0.1 broadcast_bitcast_fusion.2
  1.1 0.3 copy.35
  1.4 2.5 %broadcast_select_fusion = bf16[8,512,384]{2,1,0:T(8,128)(2,1)S(1)} fusion(bf16[8,512,384]{2,1,0:T(8,128)(2,1)} %param.12, pred[512,384]{1,0:T(8,128)(4,1)S(1)} %copy.35), kind=kLoop, calls=%fused_computation.26 | loop fusion | flops 1572864 | bytes 6488064 | tf_op jit(solution)/shard_map/jit(_where)/select_n | solution.py:41
  3.9 1.4 fusion.43
  5.2 3.2 %collective-permute-start.1 = (bf16[8,128,384]{2,1,0:T(8,128)(2,1)}, bf16[8,128,384]{2,1,0:T(8,128)(2,1)}, u32[]{:S(2)}, u32[]{:S(2)}) collective-permute-start(bf16[8,128,384]{2,1,0:T(8,128)(2,1)} %get-tuple-element.44), channel_id=1, source_target_pairs={{0,4},{4,8},{8,12},{12,16},{16,20},{20,24},{24,28},{1,5},{5,9},{9,... | collective-permute-start | bytes 2359304 | tf_op jit(solution)/shard_map/ppermute | solution.py:12
  8.5 1.3 collective-permute-start.2
  9.8 0.1 copy.36
  9.9 0.1 broadcast_bitcast_fusion.1
  10.0 1.9 %copy.37 = bf16[512,384]{0,1:T(8,128)(2,1)} copy(bf16[512,384]{1,0:T(8,128)(2,1)} %param.16) | data formatting | bytes 786432 | tf_op args[4]
  11.9 1.0 bitcast_select_fusion.2
  12.9 0.7 fusion.44
  13.6 5.0 %collective-permute-start = (bf16[128,384]{0,1:T(8,128)(2,1)}, bf16[128,384]{0,1:T(8,128)(2,1)}, u32[]{:S(2)}, u32[]{:S(2)}) collective-permute-start(bf16[128,384]{0,1:T(8,128)(2,1)} %get-tuple-element.47), channel_id=1, source_target_pairs={{0,4},{4,8},{8,12},{12,16},{16,20},{20,24},{24,28},{1,5},{5,9},{9,... | collective-permute-start | bytes 294920 | tf_op jit(solution)/shard_map/ppermute | solution.py:12
  18.6 1.3 collective-permute-start.3
  19.9 5.4 %copy.55 = bf16[8,512,384]{2,0,1:T(8,128)(2,1)} copy(bf16[8,512,384]{2,1,0:T(8,128)(2,1)} %param.12) | data formatting | bytes 6291456 | tf_op args[0]
  25.4 4.7 %all-to-all-start.1 = ((bf16[8,512,384]{2,0,1:T(8,128)(2,1)}), bf16[8,512,384]{2,0,1:T(8,128)(2,1)}, u32[]{:S(2)}, u32[]{:S(2)}) async-start(bf16[8,512,384]{2,0,1:T(8,128)(2,1)} %copy.55), calls=%async_computation.1 | async-start | bytes 6291456 | tf_op jit(solution)/shard_map/all_to_all | solution.py:39
  30.0 0.1 copy.39
  30.1 0.1 broadcast_bitcast_fusion
  30.2 1.9 %copy.40 = bf16[512,384]{0,1:T(8,128)(2,1)} copy(bf16[512,384]{1,0:T(8,128)(2,1)} %param.14) | data formatting | bytes 786432 | tf_op args[2]
  32.2 1.0 bitcast_select_fusion.1
  33.2 0.8 fusion.45
  34.0 0.9 copy.75
  34.9 1.7 copy.41
  36.5 1.7 copy.43
  38.2 1.7 copy.45
  39.9 1.9 %pad_maximum_fusion.4 = (bf16[512,384]{0,1:T(8,128)(2,1)}, bf16[512,384]{0,1:T(8,128)(2,1)}) fusion(bf16[512,384]{0,1:T(8,128)(2,1)S(1)} %bitcast_select_fusion.2, bf16[128,384]{0,1:T(8,128)(2,1)} %collective-permute-done, bf16[128,384]{0,1:T(8,128)(2,1)} %collective-permute-done.3), kind=kLoop, calls=%fused_computation.35 | loop fusion | flops 1572864 | bytes 1376256 | tf_op jit(solution)/shard_map/concatenate | solution.py:16
  41.8 1.2 copy.38
  43.0 1.9 %copy.50 = bf16[512,384]{1,0:T(8,128)(2,1)} copy(bf16[512,384]{0,1:T(8,128)(2,1)} %get-tuple-element.46) | data formatting | bytes 786432 | tf_op jit(solution)/shard_map/slice | solution.py:57
  44.9 3.1 %pad_maximum_fusion.1 = (bf16[8,512,384]{2,1,0:T(8,128)(2,1)}, bf16[8,512,384]{2,1,0:T(8,128)(2,1)S(1)}) fusion(bf16[8,128,384]{2,1,0:T(8,128)(2,1)} %collective-permute-done.2, bf16[8,512,384]{2,1,0:T(8,128)(2,1)S(1)} %broadcast_select_fusion, bf16[8,128,384]{2,1,0:T(8,128)(2,1)} %collective-permute-done.1), kind=kLoop, calls=%fused_computation.13 | loop fusion | flops 12582912 | bytes 11010048 | tf_op jit(solution)/shard_map/concatenate | solution.py:16
  48.0 1.2 fusion.24
  49.3 1.5 scatter-add.10
  50.8 3.3 %fusion.2 = f32[8,4,128,640]{2,3,0,1:T(8,128)S(1)} fusion(f32[8,4,128,640]{2,3,0,1:T(8,128)S(1)} %scatter-add.10, bf16[4,128,128,1]{2,1,3,0:T(8,128)(2,1)S(1)} %bitcast.111, bf16[8,4,128,384]{3,2,1,0:T(8,128)(2,1)S(1)} %bitcast.104), kind=kOutput, calls=%fused_computation.6 | convolution fusion | flops 404226048 | bytes 15859712 | tf_op jit(solution)/shard_map/jin,qjnk->qjik/dot_general | solution.py:51
  54.1 3.3 %fusion = f32[8,4,128,640]{2,3,0,1:T(8,128)S(1)} fusion(f32[8,4,128,640]{2,3,0,1:T(8,128)S(1)} %fusion.2, bf16[4,128,128,1]{2,1,3,0:T(8,128)(2,1)S(1)} %bitcast.110, bf16[8,4,128,384]{3,2,1,0:T(8,128)(2,1)S(1)} %bitcast.106), kind=kOutput, calls=%fused_computation.1 | convolution fusion | flops 404226048 | bytes 15859712 | tf_op jit(solution)/shard_map/jin,qjnk->qjik/dot_general | solution.py:51
  57.3 3.1 %convert_element_type.6 = bf16[8,4,128,640]{2,3,0,1:T(8,128)(2,1)} convert(f32[8,4,128,640]{2,3,0,1:T(8,128)S(1)} %fusion) | non-fusion elementwise | flops 2621440 | bytes 15728640 | tf_op jit(solution)/shard_map/convert_element_type | solution.py:53
  60.5 2.8 %fusion.27 = bf16[8,4,128,128]{2,3,0,1:T(8,128)(2,1)S(1)} fusion(bf16[4,128,384,1]{2,1,3,0:T(8,128)(2,1)S(1)} %bitcast.114, bf16[8,4,128,640]{2,3,0,1:T(8,128)(2,1)} %convert_element_type.6), kind=kOutput, calls=%fused_computation.28 | convolution fusion | flops 402653184 | bytes 4587520 | tf_op jit(solution)/shard_map/qjik,jlk->qjil/dot_general | solution.py:59
  63.2 2.7 %fusion.33 = bf16[8,4,128,128]{2,3,0,1:T(8,128)(2,1)S(1)} fusion(bf16[4,128,384,1]{2,1,3,0:T(8,128)(2,1)S(1)} %bitcast.115, bf16[8,4,128,640]{2,3,0,1:T(8,128)(2,1)} %convert_element_type.6), kind=kOutput, calls=%fused_computation.30 | convolution fusion | flops 402653184 | bytes 4587520 | tf_op jit(solution)/shard_map/qjik,jlk->qjil/dot_general | solution.py:59
  65.9 0.7 fusion.30
  66.7 0.3 pad_maximum_fusion
  67.0 2.8 %copy.52 = bf16[8,4,128,384]{3,2,1,0:T(8,128)(2,1)} copy(bf16[8,4,128,384]{2,3,0,1:T(8,128)(2,1)S(1)} %pad_maximum_fusion) | data formatting | bytes 6291456 | tf_op jit(solution)/shard_map/concatenate | solution.py:66
  69.8 2.5 %fusion.1 = bf16[8,512,384]{2,1,0:T(8,128)(2,1)S(1)} fusion(bf16[8,4,128,384]{3,2,1,0:T(8,128)(2,1)} %copy.52, pred[512,384]{1,0:T(8,128)(4,1)S(1)} %copy-done.3), kind=kLoop, calls=%fused_computation.4 | loop fusion | flops 1572864 | bytes 6488064 | tf_op jit(solution)/shard_map/convert_element_type | solution.py:67
  72.4 3.5 %copy.53 = bf16[8,512,384]{2,0,1:T(8,128)(2,1)} copy(bf16[8,512,384]{2,1,0:T(8,128)(2,1)S(1)} %fusion.1) | data formatting | bytes 6291456 | tf_op jit(solution)/shard_map/convert_element_type | solution.py:67
  75.9 4.2 %all-to-all-start = ((bf16[8,512,384]{2,0,1:T(8,128)(2,1)}), bf16[8,512,384]{2,0,1:T(8,128)(2,1)S(1)}, u32[]{:S(2)}, u32[]{:S(2)}) async-start(bf16[8,512,384]{2,0,1:T(8,128)(2,1)} %copy.53), calls=%async_computation | async-start | bytes 6291456 | tf_op jit(solution)/shard_map/all_to_all | solution.py:68
  80.0 37.2 %all-to-all-done = bf16[8,512,384]{2,0,1:T(8,128)(2,1)S(1)} async-done(((bf16[8,512,384]{2,0,1:T(8,128)(2,1)}), bf16[8,512,384]{2,0,1:T(8,128)(2,1)S(1)}, u32[]{:S(2)}, u32[]{:S(2)}) %all-to-all-start) | async-done | bytes 3145760 | tf_op jit(solution)/shard_map/all_to_all | solution.py:68
  117.3 2.8 %fusion.36 = f32[32,32]{0,1:T(8,128)S(1)} fusion(bf16[8,4,128,384]{3,0,2,1:T(8,128)(2,1)} %bitcast.34, bf16[8,4,128,384]{3,0,2,1:T(8,128)(2,1)S(1)} %bitcast.107), kind=kOutput, calls=%fused_computation.31 | convolution fusion | flops 100663296 | bytes 6295552 | tf_op jit(solution)/shard_map/dot_general | solution.py:69
  120.1 0.1 copy.57
  120.2 68.7 %all-gather = f32[1024,32]{1,0:T(8,128)S(1)} all-gather(f32[32,32]{1,0:T(8,128)S(1)} %copy.57), channel_id=2, replica_groups=mesh['orb'=8,'aux'=4] {'orb','aux'}, dimensions={0}, use_global_device_ids=true | all-gather | bytes 135168 | tf_op jit(solution)/shard_map/all_gather | solution.py:72
  188.9 0.6 constant_dynamic-slice_fusion
  (29 shorter events, 0.2 us)
Async XLA Ops:
  1.4 2.5 %copy-start.2 = (pred[512,384]{1,0:T(8,128)(4,1)}, pred[512,384]{1,0:T(8,128)(4,1)S(1)}, u32[]{:S(2)}) copy-start(pred[512,384]{1,0:T(8,128)(4,1)S(1)} %copy.35) | copy-start | bytes 589828
  5.2 39.7 %collective-permute-start.1 = (bf16[8,128,384]{2,1,0:T(8,128)(2,1)}, bf16[8,128,384]{2,1,0:T(8,128)(2,1)}, u32[]{:S(2)}, u32[]{:S(2)}) collective-permute-start(bf16[8,128,384]{2,1,0:T(8,128)(2,1)} %get-tuple-element.44), channel_id=1, source_target_pairs={{0,4},{4,8},{8,12},{12,16},{16,20},{20,24},{24,28},{1,5},{5,9},{9,... | collective-permute-start | bytes 2359304 | tf_op jit(solution)/shard_map/ppermute | solution.py:12
  8.5 36.4 %collective-permute-start.2 = (bf16[8,128,384]{2,1,0:T(8,128)(2,1)}, bf16[8,128,384]{2,1,0:T(8,128)(2,1)}, u32[]{:S(2)}, u32[]{:S(2)}) collective-permute-start(bf16[8,128,384]{2,1,0:T(8,128)(2,1)} %get-tuple-element.43), channel_id=1, source_target_pairs={{4,0},{8,4},{12,8},{16,12},{20,16},{24,20},{28,24},{5,1},{9,5},{13... | collective-permute-start | bytes 2359304 | tf_op jit(solution)/shard_map/ppermute | solution.py:15
  13.6 26.2 %collective-permute-start = (bf16[128,384]{0,1:T(8,128)(2,1)}, bf16[128,384]{0,1:T(8,128)(2,1)}, u32[]{:S(2)}, u32[]{:S(2)}) collective-permute-start(bf16[128,384]{0,1:T(8,128)(2,1)} %get-tuple-element.47), channel_id=1, source_target_pairs={{0,4},{4,8},{8,12},{12,16},{16,20},{20,24},{24,28},{1,5},{5,9},{9,... | collective-permute-start | bytes 294920 | tf_op jit(solution)/shard_map/ppermute | solution.py:12
  18.6 21.2 %collective-permute-start.3 = (bf16[128,384]{0,1:T(8,128)(2,1)}, bf16[128,384]{0,1:T(8,128)(2,1)}, u32[]{:S(2)}, u32[]{:S(2)}) collective-permute-start(bf16[128,384]{0,1:T(8,128)(2,1)} %get-tuple-element.48), channel_id=1, source_target_pairs={{4,0},{8,4},{12,8},{16,12},{20,16},{24,20},{28,24},{5,1},{9,5},{13... | collective-permute-start | bytes 294920 | tf_op jit(solution)/shard_map/ppermute | solution.py:15
  25.4 50.5 %all-to-all-start.1 = ((bf16[8,512,384]{2,0,1:T(8,128)(2,1)}), bf16[8,512,384]{2,0,1:T(8,128)(2,1)}, u32[]{:S(2)}, u32[]{:S(2)}) async-start(bf16[8,512,384]{2,0,1:T(8,128)(2,1)} %copy.55), calls=%async_computation.1 | async-start | bytes 6291456 | tf_op jit(solution)/shard_map/all_to_all | solution.py:39
  44.9 3.1 %copy-start.6 = (bf16[512,128]{1,0:T(8,128)(2,1)S(1)}, bf16[512,128]{1,0:T(8,128)(2,1)}, u32[]{:S(2)}) copy-start(bf16[512,128]{1,0:T(8,128)(2,1)} %copy.41) | copy-start | bytes 393220
  49.3 1.5 copy-start.5
  50.8 3.3 %copy-start = (bf16[8,512,384]{2,1,0:T(8,128)(2,1)S(1)}, bf16[8,512,384]{2,1,0:T(8,128)(2,1)}, u32[]{:S(2)}) copy-start(bf16[8,512,384]{2,1,0:T(8,128)(2,1)} %get-tuple-element.41) | copy-start | bytes 9437188
  50.8 3.3 %copy-start.4 = (bf16[512,128]{1,0:T(8,128)(2,1)S(1)}, bf16[512,128]{1,0:T(8,128)(2,1)}, u32[]{:S(2)}) copy-start(bf16[512,128]{1,0:T(8,128)(2,1)} %copy.45) | copy-start | bytes 393220
  60.5 2.8 %copy-start.8 = (bf16[512,384]{1,0:T(8,128)(2,1)S(1)}, bf16[512,384]{1,0:T(8,128)(2,1)}, u32[]{:S(2)}) copy-start(bf16[512,384]{1,0:T(8,128)(2,1)} %copy.50) | copy-start | bytes 1179652
  60.5 5.5 %copy-start.1 = (bf16[8,4,128,640]{2,3,0,1:T(8,128)(2,1)S(1)}, bf16[8,4,128,640]{2,3,0,1:T(8,128)(2,1)}, u32[]{:S(2)}) copy-start(bf16[8,4,128,640]{2,3,0,1:T(8,128)(2,1)} %convert_element_type.6) | copy-start | bytes 15728644
  63.2 2.7 %copy-start.7 = (bf16[512,384]{1,0:T(8,128)(2,1)S(1)}, bf16[512,384]{1,0:T(8,128)(2,1)}, u32[]{:S(2)}) copy-start(bf16[512,384]{1,0:T(8,128)(2,1)} %copy.75) | copy-start | bytes 1179652
  67.0 2.8 %copy-start.3 = (pred[512,384]{1,0:T(8,128)(4,1)S(1)}, pred[512,384]{1,0:T(8,128)(4,1)}, u32[]{:S(2)}) copy-start(pred[512,384]{1,0:T(8,128)(4,1)} %copy-done.2) | copy-start | bytes 589828
  75.9 41.4 %all-to-all-start = ((bf16[8,512,384]{2,0,1:T(8,128)(2,1)}), bf16[8,512,384]{2,0,1:T(8,128)(2,1)S(1)}, u32[]{:S(2)}, u32[]{:S(2)}) async-start(bf16[8,512,384]{2,0,1:T(8,128)(2,1)} %copy.53), calls=%async_computation | async-start | bytes 6291456 | tf_op jit(solution)/shard_map/all_to_all | solution.py:68
